TPU v7x, 32 devices: a whole 2x2x4 slice. The times are simulated.
32 devices in a mesh: dp: 16 (over z, x, core), factor: 2 (over y).
Axes of the slice: x: 2, y: 2, z: 4, core: 2. Of those that a mesh axis runs over, the one named last changes fastest.
Arguments:
- activations: bfloat16 [32768, 14336], P('dp', 'factor'), may hold values from -6 to 6
- out_grads: bfloat16 [32768, 4096], P('dp', 'factor'), may hold values from -6 to 6
- proj_in: bfloat16 [14336, 256], P('factor'), may hold values from -0.046875 to 0.046875
- proj_out: bfloat16 [4096, 256], P('factor'), may hold values from -0.09375 to 0.09375
- basis_in: bfloat16 [256, 256], replicated, may hold values from -0.375 to 0.375
- basis_out: bfloat16 [256, 256], replicated, may hold values from -0.375 to 0.375
- eigen_values: float32 [256, 256], P('factor'), may hold values from 0.01 to 10
- query_in: bfloat16 [128, 8, 256], P('dp'), may hold values from -3 to 3
- query_out: bfloat16 [128, 8, 256], P('dp'), may hold values from -3 to 3
- lengths: int32 [16, 16], P('dp'), may hold values from 1 to 256, 2048 in all within a row
- continues: int32 [16], replicated, may hold values from 0 to 1, as said below
- owners: int32 [256, 1], replicated, may hold values from 0 to 15; in each aligned block of 256 rows (0 to 255, 256 to 511, ...) at most 32 rows name the same one
Outputs:
- influence: float32 [512, 128], P('dp')
Inputs may be any that keep to these rules, and one draw needn't show every extreme that they name: `lengths`: each row sums to 2048. `continues`: the flags of sequences 0, 7, 8 and 14 are 1; the flag of the last sequence is not read. `owners`: no dp index owns more than 32 document numbers, and one owns exactly 32.
All inputs are finite; a program needn't handle non-finite values.
Results may differ from a plain program's by a relative error of at most 0.0027.
Values may be sent and summed in bfloat16 or wider, within the bound.
A program may use at most 128 MiB of HBM per device.

v0:
```python
import jax
import jax.numpy as jnp
from jax import lax
from jax.sharding import PartitionSpec as P

OWN_CAP = 32
MOST_LEN = 256
DAMPING = 0.1
EPSILON = 1e-06
F32 = jnp.float32
BF16 = jnp.bfloat16


def dot(a, b):
    return jnp.dot(a, b, preferred_element_type=F32)


def exact_right(x, basis):
    return jnp.dot(x, basis.astype(F32), precision=lax.Precision.HIGH)


def window_of(tokens, shards):
    share = tokens // shards
    if shards == 1:
        return tokens
    return min(tokens, share + (MOST_LEN // 2 if shards == 2 else MOST_LEN))


def window_start(index, tokens, shards):
    window = window_of(tokens, shards)
    return jnp.clip(index * (tokens // shards) - MOST_LEN // 2, 0, tokens - window)


def summed_window(activations, out_grads, proj_in, proj_out, tokens, shards):
    window = window_of(tokens, shards)
    here = lax.axis_index("factor")
    parts = jnp.concatenate([dot(activations, proj_in), dot(out_grads, proj_out)], axis=1)
    total = lax.dynamic_slice_in_dim(parts, window_start(here, tokens, shards), window, 0)
    for step in range(1, shards):
        to = lax.rem(here + step, shards)
        block = lax.dynamic_slice_in_dim(parts, window_start(to, tokens, shards), window, 0)
        route = [(i, (i + step) % shards) for i in range(shards)]
        total = total + lax.ppermute(block.astype(BF16), "factor", route).astype(F32)
    return total


def per_device(
    activations,
    out_grads,
    proj_in,
    proj_out,
    basis_in,
    basis_out,
    eigen_values,
    query_in,
    query_out,
    lengths,
    continues,
    owners,
):
    tokens = activations.shape[0]
    pieces = lengths.shape[1]
    rank_in = basis_in.shape[0]
    factor_index = lax.axis_index("factor")
    shards = lax.axis_size("factor")
    data_index = lax.axis_index("dp")
    data_count = lax.axis_size("dp")
    highest = lax.Precision.HIGHEST
    window = window_of(tokens, shards)
    first_row = window_start(factor_index, tokens, shards)

    both = jnp.concatenate([query_in, query_out], axis=2)
    both = lax.all_gather(both, "dp", axis=0, tiled=True)
    queries, query_tokens, _ = both.shape
    both = both.reshape(queries * query_tokens, -1)
    q_in = dot(both[:, :rank_in], basis_in)
    q_out = dot(both[:, rank_in:], basis_out)
    eigen = lax.all_gather(eigen_values, "factor", axis=0, tiled=True)
    scale = 1.0 / (eigen + DAMPING)

    total = summed_window(activations, out_grads, proj_in, proj_out, tokens, shards)
    rot_in = exact_right(total[:, :rank_in], basis_in)
    rot_out = exact_right(total[:, rank_in:], basis_out)

    piece_lengths = lengths[0]
    upto = jnp.arange(pieces)[:, None] <= jnp.arange(pieces)[None, :]
    piece_ends = jnp.sum(jnp.where(upto, piece_lengths[:, None], 0), axis=0)
    piece_starts = piece_ends - piece_lengths
    mine = ((piece_starts + piece_ends) // 2) // (tokens // shards) == factor_index

    pad = ((0, MOST_LEN), (0, 0))
    rot_in, rot_out = jnp.pad(rot_in, pad), jnp.pad(rot_out, pad)
    at = jnp.clip(piece_starts - first_row, 0, window)
    row = jnp.arange(MOST_LEN)[None, :]
    inside = (row < piece_lengths[:, None]) & mine[:, None]

    def cut(x):
        return jnp.stack([lax.dynamic_slice_in_dim(x, at[k], MOST_LEN, 0) for k in range(pieces)])

    in_cut = jnp.where(inside[:, :, None], cut(rot_in), 0)
    grads = jnp.einsum("pto,pti->poi", cut(rot_out), in_cut, precision=lax.Precision.HIGH)
    linear = [(s * shards + shards - 1, (s + 1) * shards) for s in range(data_count - 1)]
    preceding = lax.ppermute(grads[pieces - 1].astype(BF16), ("dp", "factor"), linear).astype(F32)
    joined_next = jnp.where(data_index < data_count - 1, continues[data_index], 0).astype(F32)
    joined_prev = jnp.where(data_index > 0, continues[jnp.maximum(data_index - 1, 0)], 0)
    grads = grads.at[0].add(joined_prev.astype(F32) * preceding)
    grads = grads.at[pieces - 1].multiply(1.0 - joined_next)
    scaled = grads * scale[None]
    self_total = jnp.sum(grads * scaled, axis=(1, 2))
    half = jnp.einsum("poi,to->pti", scaled, q_out, precision=lax.Precision.HIGH)
    raw = jnp.sum((half * q_in[None]).reshape(pieces, queries, -1), axis=2)
    relative = raw / jnp.sqrt(self_total + EPSILON)[:, None]

    everyone = lax.all_gather(relative, ("dp", "factor"), axis=0, tiled=True)
    own_all = owners[:, 0]
    numbers = jnp.arange(own_all.shape[0], dtype=jnp.int32)
    earlier = (own_all[None, :] == own_all[:, None]) & (numbers[None, :] < numbers[:, None])
    rank = jnp.sum(earlier.astype(jnp.int32), axis=1)
    slot = jnp.where(own_all == data_index, rank, -1)
    slot = jnp.broadcast_to(slot.reshape(data_count, 1, pieces), (data_count, shards, pieces))
    placing = jnp.arange(OWN_CAP, dtype=jnp.int32)[:, None] == slot.reshape(1, -1)
    return jnp.dot(placing.astype(F32), everyone, precision=highest)


def solution(mesh):
    placed = (
        P("dp", "factor"),
        P("dp", "factor"),
        P("factor", None),
        P("factor", None),
        P(),
        P(),
        P("factor", None),
        P("dp", None, None),
        P("dp", None, None),
        P("dp", None),
        P(),
        P(),
    )
    return jax.shard_map(
        per_device, mesh=mesh, in_specs=placed, out_specs=P("dp", None), check_vma=False
    )
```

profile of v0, /device:TPU:0, one launch (start us, length us, event | category | flops | bytes accessed | tf_op | source)
XLA Modules:
  0.0 197.3 jit_solution(15589526621846962180)
XLA Ops:
  6.5 1.5 pad_maximum_fusion
  8.1 13.9 %fusion.77 = f32[2048,256]{0,1:T(8,128)S(1)} fusion(bf16[2048,7168]{1,0:T(8,128)(2,1)} %param.16, bf16[7168,256]{1,0:T(8,128)(2,1)} %param.18), kind=kOutput, calls=%fused_computation.157 | convolution fusion | flops 7516192768 | bytes 35127296 | tf_op jit(solution)/shard_map/dot_general | solution.py:15
  22.0 5.8 %fusion.78 = f32[2048,256]{0,1:T(8,128)S(1)} fusion(bf16[2048,2048]{1,0:T(8,128)(2,1)} %param.17, bf16[2048,256]{1,0:T(8,128)(2,1)S(1)} %copy-done), kind=kOutput, calls=%fused_computation.158 | convolution fusion | flops 2147483648 | bytes 11534336 | tf_op jit(solution)/shard_map/dot_general | solution.py:15
  27.7 1.3 copy-done.3
  29.1 1.6 fusion.5
  30.7 3.0 %collective-permute-start = (bf16[1152,512]{0,1:T(8,128)(2,1)}, bf16[1152,512]{0,1:T(8,128)(2,1)}, u32[]{:S(2)}, u32[]{:S(2)}) collective-permute-start(bf16[1152,512]{0,1:T(8,128)(2,1)} %fusion.5), channel_id=1, source_target_pairs={{0,1},{1,0},{2,3},{3,2},{4,5},{5,4},{6,7},{7,6},{8,9},{9,8},{10,11... | collective-permute-start | bytes 3538952 | tf_op jit(solution)/shard_map/ppermute | solution.py:43
  33.7 0.1 select_reduce_fusion
  33.8 0.7 fusion.76
  54.4 0.7 fusion.75
  56.5 0.1 eq.56
  56.6 0.2 convert_reduce_fusion
  56.7 0.1 reduce_sum.48
  56.8 0.1 eq.61
  66.9 5.9 %all_gather.10 = f32[256,256]{1,0:T(8,128)} all-gather(f32[128,256]{1,0:T(8,128)S(1)} %copy-done.19), channel_id=1, replica_groups=mesh['dp'=16,'factor'=2] {'factor'}, dimensions={0}, use_global_device_ids=true | all-gather | bytes 393216 | tf_op jit(solution)/shard_map/all_gather | solution.py:78
  72.9 0.1 fusion.72
  73.0 2.4 %fusion.7 = f32[1152,512]{0,1:T(8,128)S(1)} fusion(s32[]{:T(128)S(6)} %min.16, f32[2048,256]{0,1:T(8,128)S(1)} %fusion.77, f32[2048,256]{0,1:T(8,128)} %copy-done.3, bf16[1152,512]{0,1:T(8,128)(2,1)} %collective-permute-done), kind=kLoop, calls=%fused_computation.13 | loop fusion | flops 1769472 | bytes 7733252 | tf_op jit(solution)/shard_map/add | solution.py:43
  75.4 0.8 fusion.11
  76.2 0.8 fusion.13
  77.0 1.3 fusion.32
  78.3 1.8 copy.143
  80.1 1.8 copy.138
  81.9 1.8 copy.139
  83.7 0.9 copy.140
  84.6 0.9 copy.141
  85.4 0.8 copy.142
  86.3 0.8 copy.129
  87.1 1.5 fusion.33
  88.6 1.1 copy.144
  89.7 1.8 copy.130
  91.5 1.8 copy.131
  93.3 1.8 copy.132
  95.1 1.8 copy.133
  96.9 0.1 copy.134
  97.0 0.1 copy.135
  97.1 0.1 copy.136
  97.3 0.1 copy.137
  97.4 1.0 constant_dynamic-update-slice_fusion.15
  98.4 0.1 fusion.35
  98.5 0.1 fusion.39
  98.6 0.1 fusion.41
  98.6 0.1 fusion.43
  98.7 0.1 fusion.45
  98.8 0.1 fusion.49
  99.5 0.5 copy-done.14
  100.0 0.1 copy-done.13
  100.1 0.1 copy-done.12
  100.2 0.1 copy-done.11
  100.4 0.1 copy-done.8
  100.5 0.1 copy-done.7
  100.6 0.1 copy-done.6
  100.7 0.1 copy-done.5
  100.8 3.0 %fusion.2 = f32[16,256,256]{2,1,0:T(8,128)S(1)} fusion(f32[16,256,256]{1,2,0:T(8,128)S(1)} %constant_dynamic-update-slice_fusion, f32[16,256,256]{2,1,0:T(8,128)S(1)} %fusion.65, pred[16,256]{1,0:T(8,128)(4,1)S(1)} %fusion.72), kind=kOutput, calls=%fused_computation.8 | convolution fusion | flops 1611661312 | bytes 12587008 | tf_op jit(solution)/shard_map/pto,pti->poi/dot_general | solution.py:101
  103.9 1.0 collective-permute-start.1
  105.0 0.1 fusion.67
  105.1 1.9 copy-done.2
  107.1 0.6 fusion.1
  107.7 1.4 fusion.15
  109.1 1.3 convolution_bitcast_fusion
  110.5 10.1 %multiply_reduce_fusion = f32[1024,16]{0,1:T(8,128)S(1)} fusion(f32[1024,256,1]{1,0,2:T(8,128)S(1)} %convolution_bitcast_fusion, f32[1024,256]{0,1:T(8,128)S(1)} %fusion.15, f32[16,256,256]{2,1,0:T(8,128)} %copy-done.2, f32[256,256]{1,0:T(8,128)S(1)} %add_divide_fusion), kind=kOutput, calls=%fused_computation | convolution fusion | flops 6451871744 | bytes 6619136 | tf_op jit(solution)/shard_map/poi,to->pti/dot_general | solution.py:110
  120.6 0.2 copy.147
  120.8 0.2 bitcast_reduce_fusion
  121.1 0.1 broadcast_divide_fusion
  121.1 68.5 %all_gather.11 = f32[512,128]{1,0:T(8,128)S(1)} all-gather(f32[16,128]{1,0:T(8,128)S(1)} %broadcast_divide_fusion), channel_id=1, replica_groups=mesh['dp'=16,'factor'=2] {'dp','factor'}, dimensions={0}, use_global_device_ids=true | all-gather | bytes 270336 | tf_op jit(solution)/shard_map/all_gather | solution.py:114
  189.7 0.8 fusion.70
  (76 shorter events, 1.2 us)
Async XLA Ops:
  6.5 15.4 %copy-start = (bf16[2048,256]{1,0:T(8,128)(2,1)S(1)}, bf16[2048,256]{1,0:T(8,128)(2,1)}, u32[]{:S(2)}) copy-start(bf16[2048,256]{1,0:T(8,128)(2,1)} %param.19) | copy-start | bytes 3145732
  6.5 101.2 %all-gather.2.cloned.1.call-start = ((), (), s32[]{:S(2)}) async-start(), calls=%async_computation | async-start | bytes 1114112 | tf_op jit(solution)/shard_map/all_gather | solution.py:73
  27.7 1.3 copy-start.3
  29.1 4.6 %copy-start.21 = (s32[1,16]{1,0:T(1,128)S(1)}, s32[1,16]{1,0:T(1,128)}, u32[]{:S(2)}) copy-start(s32[1,16]{1,0:T(1,128)} %param.25) | copy-start | bytes 196
  29.1 25.4 %copy-start.22 = (s32[16]{0:T(128)S(1)}, s32[16]{0:T(128)}, u32[]{:S(2)}) copy-start(s32[16]{0:T(128)} %param.26) | copy-start | bytes 196
  29.1 27.4 %copy-start.20 = (s32[256,1]{0,1:T(1,128)S(1)}, s32[256,1]{0,1:T(1,128)}, u32[]{:S(2)}) copy-start(s32[256,1]{0,1:T(1,128)} %param.27) | copy-start | bytes 3076
  29.1 37.8 %copy-start.19 = (f32[128,256]{1,0:T(8,128)S(1)}, f32[128,256]{1,0:T(8,128)}, u32[]{:S(2)}) copy-start(f32[128,256]{1,0:T(8,128)} %param.22) | copy-start | bytes 393220
  30.7 42.3 %collective-permute-start = (bf16[1152,512]{0,1:T(8,128)(2,1)}, bf16[1152,512]{0,1:T(8,128)(2,1)}, u32[]{:S(2)}, u32[]{:S(2)}) collective-permute-start(bf16[1152,512]{0,1:T(8,128)(2,1)} %fusion.5), channel_id=1, source_target_pairs={{0,1},{1,0},{2,3},{3,2},{4,5},{5,4},{6,7},{7,6},{8,9},{9,8},{10,11... | collective-permute-start | bytes 3538952 | tf_op jit(solution)/shard_map/ppermute | solution.py:43
  36.3 39.0 %copy-start.15 = (bf16[256,256]{1,0:T(8,128)(2,1)S(1)}, bf16[256,256]{1,0:T(8,128)(2,1)}, u32[]{:S(2)}) copy-start(bf16[256,256]{1,0:T(8,128)(2,1)} %param.20) | copy-start | bytes 393220
  72.9 3.3 %copy-start.17 = (bf16[256,256]{1,0:T(8,128)(2,1)S(1)}, bf16[256,256]{1,0:T(8,128)(2,1)}, u32[]{:S(2)}) copy-start(bf16[256,256]{1,0:T(8,128)(2,1)} %param.21) | copy-start | bytes 393220
  99.0 1.0 copy-start.14
  99.1 1.0 copy-start.13
  99.1 1.0 copy-start.12
  99.1 1.1 copy-start.11
  99.3 1.1 copy-start.10
  99.3 1.2 copy-start.9
  99.3 1.2 copy-start.8
  99.3 1.3 copy-start.7
  99.4 1.3 copy-start.6
  99.4 1.3 copy-start.5
  100.8 4.1 %copy-start.4 = (f32[256,256]{1,0:T(8,128)S(1)}, f32[256,256]{1,0:T(8,128)}, u32[]{:S(2)}) copy-start(f32[256,256]{1,0:T(8,128)} %all_gather.10) | copy-start | bytes 786436
  103.8 3.9 %copy-start.16 = (bf16[256,256]{1,0:T(8,128)(2,1)S(1)}, bf16[256,256]{1,0:T(8,128)(2,1)}, u32[]{:S(2)}) copy-start(bf16[256,256]{1,0:T(8,128)(2,1)} %param.20) | copy-start | bytes 393220
  103.9 5.3 %copy-start.18 = (bf16[256,256]{1,0:T(8,128)(2,1)S(1)}, bf16[256,256]{1,0:T(8,128)(2,1)}, u32[]{:S(2)}) copy-start(bf16[256,256]{1,0:T(8,128)(2,1)} %param.21) | copy-start | bytes 393220
  103.9 1.1 collective-permute-start.1
  105.1 1.9 copy-start.2
  110.5 80.0 %copy-start.1 = (bf16[2048,256]{1,0:T(8,128)(2,1)S(1)}, bf16[2048,256]{1,0:T(8,128)(2,1)}, u32[]{:S(2)}) copy-start(bf16[2048,256]{1,0:T(8,128)(2,1)} %param.19) | copy-start | bytes 3145732
Sparse Core Ops, SparseCore 0:
  9.5 40.6 all-gather.1
where the time goes:
time: 198 us; the launch traced here: 197 us
  blocking collectives  74.5 us (38%)
  between operations  45.2 us (23%)
  matrix products  37.9 us (19%)
  local copies, waits for them, and re-layouts  28.7 us (14%)
  other arithmetic  6.96 us (4%)
  starting transfers between devices  4.01 us (2%)
    all_gather x1, blocking collectives, per_device(): everyone = lax.all_gather(relative, ('dp', 'factor'), axis=0, tiled=True)  68.5 us
    dot_general x4, matrix products, dot(): return jnp.dot(a, b, preferred_element_type=F32)  22.3 us
    another operation x20, local copies, waits for them, and re-layouts, cut(): jnp.stack([lax.dynamic_slice_in_dim(x, at[k], MOST_LEN, 0) for k in range...  20.4 us
    dot_general x1, matrix products, per_device(): jnp.einsum('poi,to->pti', scaled, q_out, precision=lax.Precision.HIGH)  10.1 us
    unnamed x76, local copies, waits for them, and re-layouts  6.36 us
    all_gather x1, blocking collectives, per_device(): eigen = lax.all_gather(eigen_values, 'factor', axis=0, tiled=True)  5.93 us
  transfers between devices with their start and end apart: 3, of which 0 were waited for; matrix products, arithmetic and copies ran while one was open for 27% of the time, Pallas kernels for 0%

commit v1 on v0

--- a/solution.py
+++ b/solution.py
@@ -1,6 +1,10 @@
+import functools
+
 import jax
 import jax.numpy as jnp
 from jax import lax
+from jax.experimental import pallas as pl
+from jax.experimental.pallas import tpu as pltpu
 from jax.sharding import PartitionSpec as P
 
 OWN_CAP = 32
@@ -9,6 +13,7 @@
 EPSILON = 1e-06
 F32 = jnp.float32
 BF16 = jnp.bfloat16
+SPAN = MOST_LEN + 8
 
 
 def dot(a, b):
@@ -42,6 +47,113 @@
         route = [(i, (i + step) % shards) for i in range(shards)]
         total = total + lax.ppermute(block.astype(BF16), "factor", route).astype(F32)
     return total
+
+
+def grads_kernel(at_ref, length_ref, in_ref, out_ref, grad_ref):
+    piece = pl.program_id(0)
+    at, length = at_ref[piece], length_ref[piece]
+
+    @pl.when(length == 0)
+    def _():
+        grad_ref[...] = jnp.zeros_like(grad_ref)
+
+    @pl.when(length > 0)
+    def _():
+        base = pl.multiple_of((at >> 3) << 3, 8)
+        shift = at - base
+        row = lax.broadcasted_iota(jnp.int32, (SPAN, 1), 0)
+        inside = (row >= shift) & (row < shift + length)
+        masked = jnp.where(inside, in_ref[pl.ds(base, SPAN), :], 0.0)
+        grad_ref[0] = lax.dot_general(
+            out_ref[pl.ds(base, SPAN), :],
+            masked,
+            (((0,), (0,)), ((), ())),
+            precision=lax.Precision.HIGHEST,
+            preferred_element_type=F32,
+        )
+
+
+def piece_grads(at, length, rot_in, rot_out):
+    pieces, rows = at.shape[0], rot_in.shape[0]
+    width_in, width_out = rot_in.shape[1], rot_out.shape[1]
+    return pl.pallas_call(
+        grads_kernel,
+        grid_spec=pltpu.PrefetchScalarGridSpec(
+            num_scalar_prefetch=2,
+            grid=(pieces,),
+            in_specs=[
+                pl.BlockSpec((rows, width_in), lambda k, *_: (0, 0)),
+                pl.BlockSpec((rows, width_out), lambda k, *_: (0, 0)),
+            ],
+            out_specs=pl.BlockSpec((1, width_out, width_in), lambda k, *_: (k, 0, 0)),
+        ),
+        out_shape=jax.ShapeDtypeStruct((pieces, width_out, width_in), F32),
+        compiler_params=pltpu.CompilerParams(vmem_limit_bytes=32 * 2**20),
+    )(at, length, rot_in, rot_out)
+
+
+def deliver_kernel(data_count, shards, rows_ref, placing_ref, result_ref, held, send_sem, recv_sem):
+    count = data_count * shards
+    me = lax.axis_index("dp") * shards + lax.axis_index("factor")
+    barrier = pltpu.get_barrier_semaphore()
+
+    def target(step):
+        to = lax.rem(me + step, count)
+        return (lax.div(to, shards), lax.rem(to, shards))
+
+    def greet(step, carry):
+        pl.semaphore_signal(
+            barrier, inc=1, device_id=target(step), device_id_type=pl.DeviceIdType.MESH
+        )
+        return carry
+
+    lax.fori_loop(1, count, greet, 0)
+    pl.semaphore_wait(barrier, count - 1)
+
+    def copy(step):
+        return pltpu.make_async_remote_copy(
+            src_ref=rows_ref,
+            dst_ref=held.at[me],
+            send_sem=send_sem.at[step],
+            recv_sem=recv_sem.at[step],
+            device_id=target(step),
+            device_id_type=pl.DeviceIdType.MESH,
+        )
+
+    def send(step, carry):
+        copy(step).start()
+        return carry
+
+    def settle(step, carry):
+        copy(step).wait()
+        return carry
+
+    lax.fori_loop(1, count, send, 0)
+    held[me] = rows_ref[...]
+    lax.fori_loop(1, count, settle, 0)
+    everyone = held[...].reshape(-1, held.shape[2])
+    result_ref[...] = jnp.dot(
+        placing_ref[...], everyone, precision=lax.Precision.HIGHEST, preferred_element_type=F32
+    )
+
+
+def deliver(relative, placing, data_count, shards):
+    count = data_count * shards
+    pieces, queries = relative.shape
+    return pl.pallas_call(
+        functools.partial(deliver_kernel, data_count, shards),
+        out_shape=jax.ShapeDtypeStruct((OWN_CAP, queries), F32),
+        in_specs=[pl.BlockSpec(memory_space=pltpu.VMEM)] * 2,
+        out_specs=pl.BlockSpec(memory_space=pltpu.VMEM),
+        scratch_shapes=[
+            pltpu.VMEM((count, pieces, queries), F32),
+            pltpu.SemaphoreType.DMA((count,)),
+            pltpu.SemaphoreType.DMA((count,)),
+        ],
+        compiler_params=pltpu.CompilerParams(
+            collective_id=0, has_side_effects=True, vmem_limit_bytes=32 * 2**20
+        ),
+    )(relative, placing)
 
 
 def per_device(
@@ -65,7 +177,6 @@
     shards = lax.axis_size("factor")
     data_index = lax.axis_index("dp")
     data_count = lax.axis_size("dp")
-    highest = lax.Precision.HIGHEST
     window = window_of(tokens, shards)
     first_row = window_start(factor_index, tokens, shards)
 
@@ -88,17 +199,11 @@
     piece_starts = piece_ends - piece_lengths
     mine = ((piece_starts + piece_ends) // 2) // (tokens // shards) == factor_index
 
-    pad = ((0, MOST_LEN), (0, 0))
-    rot_in, rot_out = jnp.pad(rot_in, pad), jnp.pad(rot_out, pad)
+    pad = ((0, SPAN), (0, 0))
     at = jnp.clip(piece_starts - first_row, 0, window)
-    row = jnp.arange(MOST_LEN)[None, :]
-    inside = (row < piece_lengths[:, None]) & mine[:, None]
-
-    def cut(x):
-        return jnp.stack([lax.dynamic_slice_in_dim(x, at[k], MOST_LEN, 0) for k in range(pieces)])
-
-    in_cut = jnp.where(inside[:, :, None], cut(rot_in), 0)
-    grads = jnp.einsum("pto,pti->poi", cut(rot_out), in_cut, precision=lax.Precision.HIGH)
+    grads = piece_grads(
+        at, jnp.where(mine, piece_lengths, 0), jnp.pad(rot_in, pad), jnp.pad(rot_out, pad)
+    )
     linear = [(s * shards + shards - 1, (s + 1) * shards) for s in range(data_count - 1)]
     preceding = lax.ppermute(grads[pieces - 1].astype(BF16), ("dp", "factor"), linear).astype(F32)
     joined_next = jnp.where(data_index < data_count - 1, continues[data_index], 0).astype(F32)
@@ -111,7 +216,6 @@
     raw = jnp.sum((half * q_in[None]).reshape(pieces, queries, -1), axis=2)
     relative = raw / jnp.sqrt(self_total + EPSILON)[:, None]
 
-    everyone = lax.all_gather(relative, ("dp", "factor"), axis=0, tiled=True)
     own_all = owners[:, 0]
     numbers = jnp.arange(own_all.shape[0], dtype=jnp.int32)
     earlier = (own_all[None, :] == own_all[:, None]) & (numbers[None, :] < numbers[:, None])
@@ -119,7 +223,7 @@
     slot = jnp.where(own_all == data_index, rank, -1)
     slot = jnp.broadcast_to(slot.reshape(data_count, 1, pieces), (data_count, shards, pieces))
     placing = jnp.arange(OWN_CAP, dtype=jnp.int32)[:, None] == slot.reshape(1, -1)
-    return jnp.dot(placing.astype(F32), everyone, precision=highest)
+    return deliver(relative, placing.astype(F32), data_count, shards)
 
 
 def solution(mesh):

time: 198 us -> 114 us (0.58)
  blocking collectives: 74.5 us -> 26 us
  between operations: 45.2 us -> 14.9 us
  local copies, waits for them, and re-layouts: 28.7 us -> 3.92 us
  Pallas kernels: 0 us -> 24.4 us
  matrix products: 37.9 us -> 34 us
    all_gather x1 -> x0, blocking collectives: 68.5 us -> none  [per_device(): everyone = lax.all_gather(relative, ('dp', 'factor'), axis=0, tiled=True)]
    pallas_call x0 -> x2, Pallas kernels: none -> 24.4 us  [the longest x1 19.6 us: deliver(): pl.pallas_call(functools.partial(deliver_kernel, data_count, shards), out...]
    another operation x20 -> x0, local copies, waits for them, and re-layouts: 20.4 us -> none  [cut(): jnp.stack([lax.dynamic_slice_in_dim(x, at[k], MOST_LEN, 0) for k in range...]
    all_gather x1, blocking collectives: 5.93 us -> 26 us  [per_device(): eigen = lax.all_gather(eigen_values, 'factor', axis=0, tiled=True)]
    dot_general x2 -> x0, matrix products: 3.84 us -> none  [the longest x1 3.01 us: per_device(): jnp.einsum('pto,pti->poi', cut(rot_out), in_cut, precision=lax.Precision....]
    unnamed x76 -> x23, local copies, waits for them, and re-layouts: 6.36 us -> 2.6 us
  transfers between devices with their start and end apart: 3 -> 3, of which waited for: 0 -> 0; matrix products, arithmetic and copies ran while one was open for 27% -> 6% of each run, Pallas kernels for 0% -> 4%
where the time goes in v1:
time: 114 us; the launch traced here: 113 us
  matrix products  34 us (30%)
  blocking collectives  26 us (23%)
  Pallas kernels  24.4 us (21%)
  between operations  14.9 us (13%)
  other arithmetic  6.1 us (5%)
  local copies, waits for them, and re-layouts  3.92 us (3%)
  starting transfers between devices  3.79 us (3%)
    all_gather x1, blocking collectives, per_device(): eigen = lax.all_gather(eigen_values, 'factor', axis=0, tiled=True)  26 us
    dot_general x4, matrix products, dot(): return jnp.dot(a, b, preferred_element_type=F32)  22.4 us
    pallas_call x1, Pallas kernels, deliver(): pl.pallas_call(functools.partial(deliver_kernel, data_count, shards), out...  19.6 us
    dot_general x1, matrix products, per_device(): jnp.einsum('poi,to->pti', scaled, q_out, precision=lax.Precision.HIGH)  10.1 us
    pallas_call x1, Pallas kernels, piece_grads(): pl.pallas_call(grads_kernel, grid_spec=pltpu.PrefetchScalarGridSpec(num_s...  4.81 us
    ppermute x1, starting transfers between devices, summed_window(): lax.ppermute(block.astype(BF16), 'factor', route).astype(F32)  2.94 us
    unnamed x23, local copies, waits for them, and re-layouts  2.6 us
    add x1, other arithmetic, summed_window(): total + lax.ppermute(block.astype(BF16), 'factor', route).astype(F32)  2.44 us
  transfers between devices with their start and end apart: 3, of which 0 were waited for; matrix products, arithmetic and copies ran while one was open for 6% of the time, Pallas kernels for 4%

profile of v1, /device:TPU:0, one launch (start us, length us, event | category | flops | bytes accessed | tf_op | source)
XLA Modules:
  0.0 113.1 jit_solution(5678755337743100143)
XLA Ops:
  6.5 0.0 copy-start
  6.5 0.0 all-gather.2.cloned.1.call-start
  6.5 13.9 %fusion.20 = f32[2048,256]{0,1:T(8,128)S(1)} fusion(bf16[2048,7168]{1,0:T(8,128)(2,1)} %param.16, bf16[7168,256]{1,0:T(8,128)(2,1)} %param.18), kind=kOutput, calls=%fused_computation.52 | convolution fusion | flops 7516192768 | bytes 35127296 | tf_op jit(solution)/shard_map/dot_general | solution.py:20
  20.4 0.0 copy-done
  20.4 5.8 %fusion.21 = f32[2048,256]{0,1:T(8,128)S(1)} fusion(bf16[2048,2048]{1,0:T(8,128)(2,1)} %param.17, bf16[2048,256]{1,0:T(8,128)(2,1)S(1)} %copy-done), kind=kOutput, calls=%fused_computation.53 | convolution fusion | flops 2147483648 | bytes 11534336 | tf_op jit(solution)/shard_map/dot_general | solution.py:20
  26.2 0.0 copy-start.2
  26.2 0.0 copy-start.6
  26.2 0.0 copy-start.7
  26.2 0.0 copy-start.9
  26.2 0.0 copy-start.8
  26.3 0.0 copy-start.5
  26.3 0.0 copy-start.10
  26.3 1.6 %fusion.3 = bf16[1152,512]{0,1:T(8,128)(2,1)} fusion(s32[]{:T(128)S(6)} %min.19, f32[2048,256]{0,1:T(8,128)S(1)} %fusion.20, f32[2048,256]{0,1:T(8,128)S(1)} %fusion.21), kind=kLoop, calls=%fused_computation.9 | loop fusion | flops 2359296 | bytes 5373956 | tf_op jit(solution)/shard_map/convert_element_type | solution.py:48
  27.9 0.0 copy-done.2
  27.9 2.9 %collective-permute-start = (bf16[1152,512]{0,1:T(8,128)(2,1)}, bf16[1152,512]{0,1:T(8,128)(2,1)}, u32[]{:S(2)}, u32[]{:S(2)}) collective-permute-start(bf16[1152,512]{0,1:T(8,128)(2,1)} %fusion.3), channel_id=1, source_target_pairs={{0,1},{1,0},{2,3},{3,2},{4,5},{5,4},{6,7},{7,6},{8,9},{9,8},{10,11... | collective-permute-start | bytes 3538952 | tf_op jit(solution)/shard_map/ppermute | solution.py:48
  30.9 0.0 copy-done.6
  30.9 0.0 copy-done.7
  30.9 0.6 pad_maximum_fusion
  31.5 0.0 all-gather.2.cloned.1.call-update
  31.5 0.0 copy-done.9
  31.6 0.6 fusion.19
  33.4 0.0 copy-done.8
  33.4 0.1 eq.54
  33.5 0.2 convert_reduce_fusion
  33.7 0.1 reduce_sum.54
  33.8 0.1 eq.59
  33.9 0.0 copy-done.5
  33.9 26.0 %all_gather.7 = f32[256,256]{1,0:T(8,128)S(1)} all-gather(f32[128,256]{1,0:T(8,128)S(1)} %copy-done.5), channel_id=1, replica_groups=mesh['dp'=16,'factor'=2] {'factor'}, dimensions={0}, use_global_device_ids=true | all-gather | bytes 393216 | tf_op jit(solution)/shard_map/all_gather | solution.py:189
  59.9 0.0 copy-done.10
  59.9 0.1 select_reduce_fusion
  60.0 0.0 copy-start.4
  60.0 0.0 collective-permute-done
  60.0 2.4 %fusion.5 = f32[1152,512]{0,1:T(8,128)S(1)} fusion(s32[]{:T(128)S(6)} %min.16, f32[2048,256]{0,1:T(8,128)S(1)} %fusion.20, f32[2048,256]{0,1:T(8,128)} %copy-done.2, bf16[1152,512]{0,1:T(8,128)(2,1)} %collective-permute-done), kind=kLoop, calls=%fused_computation.11 | loop fusion | flops 1769472 | bytes 7733252 | tf_op jit(solution)/shard_map/add | solution.py:48
  62.5 0.0 copy-done.4
  62.5 0.0 copy-start.3
  62.5 0.8 fusion.9
  63.3 0.1 pad.11.in_ref
  63.4 0.0 copy-done.3
  63.4 0.8 fusion.7
  64.2 0.1 pad.12.out_ref
  64.3 4.8 %shard_map.118 = f32[16,256,256]{2,1,0:T(8,128)S(1)} custom-call(s32[16]{0:T(128)S(1)} %get-tuple-element.30.at_ref, s32[16]{0:T(128)S(1)} %get-tuple-element.29.length_ref, f32[1416,256]{1,0:T(8,128)S(1)} %pad.11.in_ref, f32[1416,256]{1,0:T(8,128)S(1)} %pad.12.out_ref), custom_call_target="tpu_custom_call" | custom-call | tf_op jit(solution)/shard_map/pallas_call | solution.py:79
  69.2 0.8 collective-permute-start.1
  70.1 0.0 collective-permute-done.1
  70.1 0.1 fusion.15
  70.2 0.0 copy-start.1
  70.2 1.9 %copy-done.1 = f32[16,256,256]{2,1,0:T(8,128)} copy-done((f32[16,256,256]{2,1,0:T(8,128)}, f32[16,256,256]{2,1,0:T(8,128)S(1)}, u32[]{:S(2)}) %copy-start.1) | copy-done | bytes 4194328
  72.1 0.7 fusion.1
  72.8 0.0 all-gather.2.cloned.1.call-done
  72.8 1.3 %convolution_bitcast_fusion = f32[1024,256,1]{1,0,2:T(8,128)S(1)} fusion(bf16[256,256]{1,0:T(8,128)(2,1)S(1)} %copy-done.3, bf16[1024,512]{1,0:T(8,128)(2,1)} %bitcast.25), kind=kOutput, calls=%fused_computation.13 | convolution fusion | flops 134217728 | bytes 1703936 | tf_op jit(solution)/shard_map/dot_general | solution.py:20
  74.1 1.4 %fusion.11 = f32[1024,256]{0,1:T(8,128)S(1)} fusion(bf16[256,256]{1,0:T(8,128)(2,1)S(1)} %copy-done.4, bf16[1024,512]{1,0:T(8,128)(2,1)} %bitcast.26), kind=kOutput, calls=%fused_computation.18 | convolution fusion | flops 134217728 | bytes 1703936 | tf_op jit(solution)/shard_map/dot_general | solution.py:20
  75.5 10.1 %multiply_reduce_fusion = f32[1024,16]{0,1:T(8,128)S(1)} fusion(f32[1024,256,1]{1,0,2:T(8,128)S(1)} %convolution_bitcast_fusion, f32[1024,256]{0,1:T(8,128)S(1)} %fusion.11, f32[16,256,256]{2,1,0:T(8,128)} %copy-done.1, f32[256,256]{1,0:T(8,128)S(1)} %add_divide_fusion), kind=kOutput, calls=%fused_computation | convolution fusion | flops 6451871744 | bytes 6619136 | tf_op jit(solution)/shard_map/poi,to->pti/dot_general | solution.py:215
  85.6 0.2 copy.26
  85.8 0.2 bitcast_reduce_fusion
  86.0 0.1 copy.27
  86.0 0.1 broadcast_divide_fusion.rows_ref
  86.1 19.6 %shard_map.119 = f32[32,128]{1,0:T(8,128)S(1)} custom-call(f32[16,128]{1,0:T(8,128)S(1)} %broadcast_divide_fusion.rows_ref, f32[32,512]{1,0:T(8,128)S(1)} %fusion.18.placing_ref), custom_call_target="tpu_custom_call" | custom-call | tf_op jit(solution)/shard_map/pallas_call | solution.py:143
  105.7 0.6 copy.33
  (9 shorter events, 0.2 us)
Async XLA Ops:
  6.5 13.9 %copy-start = (bf16[2048,256]{1,0:T(8,128)(2,1)S(1)}, bf16[2048,256]{1,0:T(8,128)(2,1)}, u32[]{:S(2)}) copy-start(bf16[2048,256]{1,0:T(8,128)(2,1)} %param.19) | copy-start | bytes 3145732
  6.5 66.3 %all-gather.2.cloned.1.call-start = ((), (), s32[]{:S(2)}) async-start(), calls=%async_computation | async-start | bytes 1114112 | tf_op jit(solution)/shard_map/all_gather | solution.py:184
  26.2 1.7 %copy-start.2 = (f32[2048,256]{0,1:T(8,128)}, f32[2048,256]{0,1:T(8,128)S(1)}, u32[]{:S(2)}) copy-start(f32[2048,256]{0,1:T(8,128)S(1)} %fusion.21) | copy-start | bytes 6291460
  26.2 4.7 %copy-start.6 = (bf16[8,8,256]{2,1,0:T(8,128)(2,1)S(1)}, bf16[8,8,256]{2,1,0:T(8,128)(2,1)}, u32[]{:S(2)}) copy-start(bf16[8,8,256]{2,1,0:T(8,128)(2,1)} %param.24) | copy-start | bytes 98308
  26.2 4.7 %copy-start.7 = (bf16[8,8,256]{2,1,0:T(8,128)(2,1)S(1)}, bf16[8,8,256]{2,1,0:T(8,128)(2,1)}, u32[]{:S(2)}) copy-start(bf16[8,8,256]{2,1,0:T(8,128)(2,1)} %param.23) | copy-start | bytes 98308
  26.2 5.3 %copy-start.9 = (s32[16]{0:T(128)S(1)}, s32[16]{0:T(128)}, u32[]{:S(2)}) copy-start(s32[16]{0:T(128)} %param.26) | copy-start | bytes 196
  26.2 7.1 %copy-start.8 = (s32[256,1]{0,1:T(1,128)S(1)}, s32[256,1]{0,1:T(1,128)}, u32[]{:S(2)}) copy-start(s32[256,1]{0,1:T(1,128)} %param.27) | copy-start | bytes 3076
  26.3 7.6 %copy-start.5 = (f32[128,256]{1,0:T(8,128)S(1)}, f32[128,256]{1,0:T(8,128)}, u32[]{:S(2)}) copy-start(f32[128,256]{1,0:T(8,128)} %param.22) | copy-start | bytes 393220
  26.3 33.6 %copy-start.10 = (s32[1,16]{1,0:T(1,128)S(1)}, s32[1,16]{1,0:T(1,128)}, u32[]{:S(2)}) copy-start(s32[1,16]{1,0:T(1,128)} %param.25) | copy-start | bytes 196
  27.9 32.1 %collective-permute-start = (bf16[1152,512]{0,1:T(8,128)(2,1)}, bf16[1152,512]{0,1:T(8,128)(2,1)}, u32[]{:S(2)}, u32[]{:S(2)}) collective-permute-start(bf16[1152,512]{0,1:T(8,128)(2,1)} %fusion.3), channel_id=1, source_target_pairs={{0,1},{1,0},{2,3},{3,2},{4,5},{5,4},{6,7},{7,6},{8,9},{9,8},{10,11... | collective-permute-start | bytes 3538952 | tf_op jit(solution)/shard_map/ppermute | solution.py:48
  60.0 2.5 %copy-start.4 = (bf16[256,256]{1,0:T(8,128)(2,1)S(1)}, bf16[256,256]{1,0:T(8,128)(2,1)}, u32[]{:S(2)}) copy-start(bf16[256,256]{1,0:T(8,128)(2,1)} %param.20) | copy-start | bytes 393220
  62.5 0.9 copy-start.3
  69.2 0.9 collective-permute-start.1
  70.2 1.9 %copy-start.1 = (f32[16,256,256]{2,1,0:T(8,128)}, f32[16,256,256]{2,1,0:T(8,128)S(1)}, u32[]{:S(2)}) copy-start(f32[16,256,256]{2,1,0:T(8,128)S(1)} %fusion.14) | copy-start | bytes 12582916
Sparse Core Ops, SparseCore 0:
  31.7 38.2 all-gather.1
